TPU v7x, 768 devices: a whole 4x8x12 slice. The times are simulated.
768 devices in a mesh: fsdp: 128 (over y, x, z_hi, core), tensor: 6 (over z_lo).
Axes of the slice: x: 4, y: 8, z: 12 (z_hi: 2, z_lo: 6; z = z_hi * 6 + z_lo), core: 2. Of those that a mesh axis runs over, the one named last changes fastest.
Arguments:
- queries: bfloat16 [16384, 3072], P('fsdp', 'tensor'), may hold values from -6 to 6
- keys: bfloat16 [16384, 3072], P('fsdp', 'tensor'), may hold values from -6 to 6
- values: bfloat16 [16384, 3072], P('fsdp', 'tensor'), may hold values from -6 to 6
- out_weight: bfloat16 [3072, 6144], P('tensor', 'fsdp'), may hold values from -0.5 to 0.5
- cotangent: bfloat16 [16384, 6144], P('fsdp', 'tensor'), may hold values from -6 to 6
- image_ids: int32 [128, 128], P('fsdp'), may hold values from 0 to 7, never falling along the last dimension, each value on 1 to 64 neighbouring positions
Outputs:
- projected: bfloat16 [16384, 6144], P('fsdp', 'tensor')
- grad_queries: bfloat16 [16384, 3072], P('fsdp', 'tensor')
- grad_keys: bfloat16 [16384, 3072], P('fsdp', 'tensor')
- grad_values: bfloat16 [16384, 3072], P('fsdp', 'tensor')
Inputs may be any that keep to these rules, and one draw needn't show every extreme that they name: `image_ids`: 8 images on each fsdp index, numbered in order; the largest has exactly 64 patches.
All inputs are finite; a program needn't handle non-finite values.
Results may differ from a plain program's by a relative error of at most 0.015.
Values may be sent and summed in bfloat16 or wider, within the bound.
A program may use at most 32 MiB of HBM per device.

v0:
```python
import jax
import jax.numpy as jnp
from jax import lax
from jax.sharding import PartitionSpec as P

HD = 128


def attend_forward(query, key, value, same):
    scores = jnp.dot(query, key.T, preferred_element_type=jnp.float32) * HD ** (-0.5)
    scores = jnp.where(same, scores, -1e30)
    top = jnp.max(scores, axis=-1, keepdims=True)
    weights = jnp.exp(scores - top)
    probs = weights / jnp.sum(weights, axis=-1, keepdims=True)
    probs_low = probs.astype(jnp.bfloat16)
    attended = jnp.dot(probs_low, value, preferred_element_type=jnp.float32).astype(jnp.bfloat16)
    return (attended, probs)


def attend_backward(query, key, value, probs, grad_out):
    probs_low = probs.astype(jnp.bfloat16)
    grad_value = jnp.dot(probs_low.T, grad_out, preferred_element_type=jnp.float32).astype(
        jnp.bfloat16
    )
    grad_probs = jnp.dot(grad_out, value.T, preferred_element_type=jnp.float32)
    delta = jnp.sum(grad_probs * probs, axis=-1, keepdims=True)
    grad_scores = (probs * (grad_probs - delta) * HD ** (-0.5)).astype(jnp.bfloat16)
    grad_query = jnp.dot(grad_scores, key, preferred_element_type=jnp.float32).astype(jnp.bfloat16)
    grad_key = jnp.dot(grad_scores.T, query, preferred_element_type=jnp.float32).astype(
        jnp.bfloat16
    )
    return (grad_query, grad_key, grad_value)


def shards(queries, keys, values, out_weight, cotangent, image_ids):
    tok_rows, width = queries.shape
    heads_here = width // HD
    full_cot = lax.all_gather(cotangent, "tensor", axis=1, tiled=True)
    ids = image_ids[0]
    same = ids[:, None] == ids[None, :]
    pieces_att = []
    prob_list = []
    for head in range(heads_here):
        lo = head * HD
        hi = lo + HD
        attended_head, probs_head = attend_forward(
            queries[:, lo:hi], keys[:, lo:hi], values[:, lo:hi], same
        )
        pieces_att.append(attended_head)
        prob_list.append(probs_head)
    attended = jnp.concatenate(pieces_att, axis=1)
    contract = (((1,), (1,)), ((), ()))
    full_weight = lax.all_gather(out_weight, "fsdp", axis=1, tiled=True)
    partial_value = jnp.dot(attended, full_weight, preferred_element_type=jnp.float32)
    grad_attended = lax.dot_general(
        full_cot, full_weight, contract, preferred_element_type=jnp.float32
    )
    grad_attended = grad_attended.astype(jnp.bfloat16)
    projected = lax.psum_scatter(
        partial_value.astype(jnp.bfloat16), "tensor", scatter_dimension=1, tiled=True
    )
    outs_q, outs_k, outs_v = ([], [], [])
    for head in range(heads_here):
        lo = head * HD
        hi = lo + HD
        grad_q, grad_k, grad_v = attend_backward(
            queries[:, lo:hi],
            keys[:, lo:hi],
            values[:, lo:hi],
            prob_list[head],
            grad_attended[:, lo:hi],
        )
        outs_q.append(grad_q)
        outs_k.append(grad_k)
        outs_v.append(grad_v)
    joined = lambda items: jnp.concatenate(items, axis=1)
    return (projected, joined(outs_q), joined(outs_k), joined(outs_v))


def solution(mesh):
    return jax.shard_map(
        shards,
        mesh=mesh,
        in_specs=(
            P("fsdp", "tensor"),
            P("fsdp", "tensor"),
            P("fsdp", "tensor"),
            P("tensor", "fsdp"),
            P("fsdp", "tensor"),
            P("fsdp", None),
        ),
        out_specs=(
            P("fsdp", "tensor"),
            P("fsdp", "tensor"),
            P("fsdp", "tensor"),
            P("fsdp", "tensor"),
        ),
        check_vma=False,
    )
```

profile of v0, /device:TPU:6, one launch (start us, length us, event | category | flops | bytes accessed | tf_op | source)
XLA Modules:
  0.0 313.3 jit_solution(12921970852546574699)
XLA Ops:
  7.2 0.0 copy-start.2
  7.2 0.0 all-gather.5.cloned.1.call-start
  7.2 0.7 all-gather.5.cloned.1.call-update
  7.9 0.0 all-gather.3.cloned.1.call-start
  8.0 0.7 all-gather.3.cloned.1.call-update
  8.7 0.0 reduce-scatter.2.cloned.1.call-start
  8.7 1.0 fusion.73
  9.7 1.0 fusion.74
  10.7 1.0 fusion.72
  11.7 1.0 fusion.75
  12.7 1.0 convolution_convert_fusion.15
  13.7 1.0 convolution_convert_fusion.16
  14.6 1.0 convolution_convert_fusion.14
  15.6 1.0 convolution_convert_fusion.17
  16.6 54.8 %all-gather.5.cloned.1.call-done = bf16[128,6144]{1,0:T(8,128)(2,1)} async-done(((bf16[128,1024]{1,0:T(8,128)(2,1)}), bf16[128,6144]{1,0:T(8,128)(2,1)}) %all-gather.5.cloned.1.call-update) | async-done | bytes 1572880 | tf_op jit(solution)/shard_map/all_gather | solution.py:38
  71.4 177.0 %all-gather.3.cloned.1.call-done = bf16[512,6144]{0,1:T(8,128)(2,1)} async-done(((bf16[512,48]{0,1:T(8,128)(2,1)}), bf16[512,6144]{0,1:T(8,128)(2,1)}) %all-gather.3.cloned.1.call-update) | async-done | bytes 6291472 | tf_op jit(solution)/shard_map/all_gather | solution.py:53
  248.4 4.3 %convolution_convert_fusion.1 = bf16[128,512]{1,0:T(8,128)(2,1)S(1)} fusion(bf16[128,6144]{1,0:T(8,128)(2,1)} %all-gather.5.cloned.1.call-done, bf16[512,6144]{0,1:T(8,128)(2,1)} %all-gather.3.cloned.1.call-done), kind=kOutput, calls=%fused_computation.1 | convolution fusion | flops 805371904 | bytes 7995392 | tf_op jit(solution)/shard_map/dot_general | solution.py:55
  252.7 0.2 convolution_convert_fusion.3
  252.9 0.0 copy-done.2
  252.9 0.2 multiply_reduce_fusion.1
  253.1 0.2 convolution_convert_fusion.4
  253.3 0.2 multiply_reduce_fusion.2
  253.5 0.2 convolution_convert_fusion.2
  253.7 0.2 convolution_convert_fusion.5
  253.9 0.8 copy.12
  254.7 0.0 copy-start
  254.7 0.0 copy-start.1
  254.7 6.1 %convolution_convert_fusion = bf16[128,6144]{1,0:T(8,128)(2,1)} fusion(bf16[512,6144]{0,1:T(8,128)(2,1)} %all-gather.3.cloned.1.call-done, bf16[128,128]{1,0:T(8,128)(2,1)S(1)} %convolution_convert_fusion.14, bf16[128,128]{1,0:T(8,128)(2,1)S(1)} %convolution_convert_fusion.15, bf16[128,128]{1,0:T(8,128)(2,1)S(1)} %convolution_convert_fusion.16, ...), kind=kOutput, calls=%fused_computation | convolution fusion | flops 806617088 | bytes 7995392 | tf_op jit(solution)/shard_map/dot_general | solution.py:54
  260.8 0.0 reduce-scatter.2.cloned.1.call-update
  260.9 0.0 copy-done
  260.9 0.2 convolution_convert_fusion.11
  261.1 0.2 convolution_convert_fusion.12
  261.3 0.2 multiply_reduce_fusion
  261.6 0.2 convolution_convert_fusion.10
  261.8 0.2 multiply_reduce_fusion.3
  262.0 0.2 convolution_convert_fusion.13
  262.2 0.8 copy.10
  263.0 0.0 copy-done.1
  263.0 0.2 convolution_convert_fusion.7
  263.2 0.2 convolution_convert_fusion.8
  263.4 0.2 convolution_convert_fusion.6
  263.6 0.2 convolution_convert_fusion.9
  263.9 0.8 copy.11
  264.6 42.2 %reduce-scatter.2.cloned.1.call-done = bf16[128,1024]{1,0:T(8,128)(2,1)} async-done(((bf16[128,6144]{1,0:T(8,128)(2,1)}), bf16[128,1024]{1,0:T(8,128)(2,1)}) %reduce-scatter.2.cloned.1.call-update) | async-done | bytes 262160 | tf_op jit(solution)/shard_map/reduce_scatter | solution.py:59
  (11 shorter events, 0.3 us)
Async XLA Ops:
  7.2 245.7 %copy-start.2 = (bf16[128,512]{1,0:T(8,128)(2,1)S(1)}, bf16[128,512]{1,0:T(8,128)(2,1)}, u32[]{:S(2)}) copy-start(bf16[128,512]{1,0:T(8,128)(2,1)} %param.8) | copy-start | bytes 393220
  7.2 64.2 %all-gather.5.cloned.1.call-start = ((), (), s32[]{:S(2)}) async-start(), calls=%async_computation.3 | async-start | bytes 1835008 | tf_op jit(solution)/shard_map/all_gather | solution.py:38
  7.9 240.5 %all-gather.3.cloned.1.call-start = ((), (), s32[]{:S(2)}) async-start(), calls=%async_computation.1 | async-start | bytes 6340608 | tf_op jit(solution)/shard_map/all_gather | solution.py:53
  8.7 298.2 %reduce-scatter.2.cloned.1.call-start = ((), (), s32[]{:S(2)}) async-start(), calls=%async_computation.2 | async-start | bytes 1835008 | tf_op jit(solution)/shard_map/reduce_scatter | solution.py:59
  254.7 6.2 %copy-start = (bf16[128,512]{1,0:T(8,128)(2,1)S(1)}, bf16[128,512]{1,0:T(8,128)(2,1)}, u32[]{:S(2)}) copy-start(bf16[128,512]{1,0:T(8,128)(2,1)} %param.7) | copy-start | bytes 393220
  254.7 8.3 %copy-start.1 = (bf16[128,512]{1,0:T(8,128)(2,1)S(1)}, bf16[128,512]{1,0:T(8,128)(2,1)}, u32[]{:S(2)}) copy-start(bf16[128,512]{1,0:T(8,128)(2,1)} %param.6) | copy-start | bytes 393220
Sparse Core Ops, SparseCore 0:
  10.4 60.9 all-gather.4
  76.9 171.4 all-gather.2
  261.0 45.7 reduce-scatter.1
where the time goes:
time: 314 us; the launch traced here: 313 us
  waiting for transfers between devices  275 us (88%)
  matrix products  21.2 us (7%)
  between operations  14 us (4%)
    all_gather x1, waiting for transfers between devices, shards(): full_weight = lax.all_gather(out_weight, 'fsdp', axis=1, tiled=True)  177 us
    all_gather x1, waiting for transfers between devices, shards(): full_cot = lax.all_gather(cotangent, 'tensor', axis=1, tiled=True)  54.8 us
    reduce_scatter x1, waiting for transfers between devices, shards(): lax.psum_scatter(partial_value.astype(jnp.bfloat16), 'tensor', scatter_di...  42.2 us
  transfers between devices with their start and end apart: 3, of which 3 were waited for; matrix products, arithmetic and copies ran while one was open for 4% of the time, Pallas kernels for 0%

commit v1 on v0

v1 whole, which is shorter than its diff:
```python
import functools

import jax
import jax.numpy as jnp
from jax import lax
from jax.experimental import pallas as pl
from jax.experimental.pallas import tpu as pltpu
from jax.sharding import PartitionSpec as P

HD = 128
SCALE = HD ** (-0.5)
MESH = pl.DeviceIdType.MESH
NX, NY, NT = 4, 8, 6
UNIT = 16
F32 = jnp.float32
BF16 = jnp.bfloat16

NT_DIMS = (((1,), (1,)), ((), ()))
TN_DIMS = (((0,), (0,)), ((), ()))


def mod(a, n):
    return lax.rem(a + 4 * n, n)


def shift_of(slab):
    a = (slab * (5 - slab)) // 2
    m = a // 2 + a // 3
    return 3 - 5 * m + 2 * m * m


def coords(f):
    return f // 16, (f // 4) % 4, (f // 2) % 2, f % 2


def index_of(y, x, zh, c):
    return ((y * NX + x) * 2 + zh) * 2 + c


class Ring:
    def __init__(self, n, pos, device, region, send_sem, recv_sem):
        self.n, self.pos, self.device, self.region = n, pos, device, region
        self.send_sem, self.recv_sem = send_sem, recv_sem
        self.steps = n // 2

    def copy(self, d, k, origin):
        last = k == self.steps - 1
        ref = self.region(origin, d if last else None)
        i = d * self.steps + k
        return pltpu.make_async_remote_copy(
            src_ref=ref, dst_ref=ref,
            send_sem=self.send_sem(i), recv_sem=self.recv_sem(i),
            device_id=self.device(1 if d == 0 else -1), device_id_type=MESH,
        )

    def origin(self, d, k):
        return mod(self.pos - k if d == 0 else self.pos + k, self.n)

    def send(self, k):
        for d in (0, 1):
            self.copy(d, k, self.origin(d, k)).start()

    def wait(self, k):
        for d in (0, 1):
            self.copy(d, k, self.origin(d, k + 1)).wait_recv()

    def finish(self):
        for k in range(self.steps):
            for d in (0, 1):
                self.copy(d, k, self.origin(d, k)).wait_send()


def kernel(q_ref, k_ref, v_ref, wt_ref, cot_ref, ids_ref,
           proj_ref, gq_ref, gk_ref, gv_ref,
           slab, att, fr_l, fr_r, snd, part, probs,
           pre_s, pre_r, ax_s, ax_r, by_s, by_r, ay_s, ay_r, bx_s, bx_r,
           dd_s, dd_r, zr_s, zl_s, za_r, rs_s, rl_r, rr_r):
    f = lax.axis_index("fsdp")
    t = lax.axis_index("tensor")
    y, x, zh, c = coords(f)
    turn = shift_of(t)
    y2 = lax.rem(y + turn, NY)
    in_a = t // 3

    sib = f + 1 - 2 * c
    x_dev = lambda s: (index_of(y, mod(x + s, NX), zh, c), t)
    y_dev = lambda s: (index_of(mod(y + s, NY), x, zh, c), t)

    barrier = pltpu.get_barrier_semaphore()

    def greet(device):
        pl.semaphore_signal(barrier, inc=1, device_id=device, device_id_type=MESH)

    for j in range(NT):
        v = c * 32 + (y2 * 4 + x if j >= 3 else x * 8 + y2)
        greet(((64 * t + v) // 3, j))
    for s in (1, -1):
        greet(x_dev(s))
        greet(y_dev(s))
    greet((sib, t))

    @pl.when(t > 0)
    def _():
        greet((f, t - 1))

    @pl.when(t < NT - 1)
    def _():
        greet((f, t + 1))

    pl.semaphore_wait(barrier, 6 + 5 + (t + NT - 1) // NT + (2 * NT - 2 - t) // NT)

    def pre_copy(i, z):
        u = 3 * f + i
        to = u // 64
        v = u % 64
        rest = v % 32
        ya, xa = rest // 4, rest % 4
        yb, xb = rest % 8, rest // 8
        yy = in_a * ya + (1 - in_a) * yb
        xx = in_a * xa + (1 - in_a) * xb
        yd = lax.rem(yy - shift_of(to) + NY, NY)
        return pltpu.make_async_remote_copy(
            src_ref=wt_ref.at[pl.ds(i * UNIT, UNIT), :],
            dst_ref=slab.at[t, pl.ds(pl.multiple_of(v * UNIT, UNIT), UNIT), :],
            send_sem=pre_s.at[2 * i + z], recv_sem=pre_r.at[t],
            device_id=(index_of(yd, xx, z, v // 32), to), device_id_type=MESH,
        )

    for i in range(3):
        for z in (0, 1):
            pre_copy(i, z).start()

    ids_row = jnp.broadcast_to(ids_ref[...].astype(F32), (HD, HD))
    same = ids_row == ids_row.T
    for h in range(4):
        cols = slice(h * HD, (h + 1) * HD)
        s = lax.dot_general(q_ref[:, cols], k_ref[:, cols], NT_DIMS, preferred_element_type=F32) * SCALE
        s = jnp.where(same, s, -1e30)
        w = jnp.exp(s - jnp.max(s, axis=-1, keepdims=True))
        p = w / jnp.sum(w, axis=-1, keepdims=True)
        probs[h] = p
        a = jnp.dot(p.astype(BF16), v_ref[:, cols], preferred_element_type=F32)
        att[t, :, cols] = a.astype(BF16)

    def att_copy(block, s, k):
        return pltpu.make_async_remote_copy(
            src_ref=att.at[block], dst_ref=att.at[block],
            send_sem=(zr_s if s > 0 else zl_s).at[k], recv_sem=za_r.at[block],
            device_id=(f, t + s), device_id_type=MESH,
        )

    def att_wait(block):
        pltpu.make_async_remote_copy(
            src_ref=att.at[block], dst_ref=att.at[block],
            send_sem=zr_s.at[0], recv_sem=za_r.at[block],
            device_id=(f, t), device_id_type=MESH,
        ).wait_recv()

    def att_step(k):
        for s in (1, -1):
            block = t - s * k
            has = (t >= k) if s > 0 else (t + k <= NT - 1)
            room = (t < NT - 1) if s > 0 else (t > 0)
            if k > 0:
                @pl.when(has)
                def _():
                    att_wait(block)
            if k < NT - 1:
                @pl.when(has & room)
                def _():
                    att_copy(block, s, k).start()

    att_step(0)

    def rows_a(o, whole):
        base = c * 512 + (o if whole else y2) * 64
        return base if whole else base + o * UNIT

    def small_a(o, half):
        r = pl.ds(pl.multiple_of(c * 512 + y2 * 64 + o * UNIT, UNIT), UNIT)
        w = slice(None) if half is None else pl.ds(half * 256, 256)
        return slab.at[pl.ds(3, 3), r, w]

    def small_b(o, half):
        r = pl.ds(pl.multiple_of(c * 512 + x * 128 + lax.rem(o + turn, NY) * UNIT, UNIT), UNIT)
        w = slice(None) if half is None else pl.ds(half * 256, 256)
        return slab.at[pl.ds(0, 3), r, w]

    def big_a(j, o, half):
        r = pl.ds(pl.multiple_of(c * 512 + lax.rem(o + turn, NY) * 64, 64), 64)
        w = slice(None) if half is None else pl.ds(half * 256, 256)
        return slab.at[j, r, w]

    def big_b(j, o, half):
        r = pl.ds(pl.multiple_of(c * 512 + o * 128, 128), 128)
        w = slice(None) if half is None else pl.ds(half * 256, 256)
        return slab.at[j, r, w]

    ax = Ring(NX, x, x_dev, small_a, lambda i: ax_s.at[i], lambda i: ax_r.at[i])
    by = Ring(NY, y, y_dev, small_b, lambda i: by_s.at[i], lambda i: by_r.at[i])
    ay = [Ring(NY, y, y_dev, functools.partial(big_a, 5 - s),
               lambda i, s=s: ay_s.at[s, i], lambda i, s=s: ay_r.at[s, i]) for s in range(3)]
    bx = [Ring(NX, x, x_dev, functools.partial(big_b, s),
               lambda i, s=s: bx_s.at[s, i], lambda i, s=s: bx_r.at[s, i]) for s in range(3)]

    to_sib = []

    def share(j, ref):
        i = sum(1 for jj, _ in to_sib if jj == j)
        cp = pltpu.make_async_remote_copy(
            src_ref=ref, dst_ref=ref, send_sem=dd_s.at[j, i], recv_sem=dd_r.at[j],
            device_id=(sib, t), device_id_type=MESH,
        )
        cp.start()
        to_sib.append((j, cp))

    def shared(j):
        half = slab.at[j, pl.ds(pl.multiple_of((1 - c) * 512, 512), 512), :]
        pltpu.make_async_remote_copy(
            src_ref=half, dst_ref=half, send_sem=dd_s.at[j, 0], recv_sem=dd_r.at[j],
            device_id=(sib, t), device_id_type=MESH,
        ).wait_recv()

    def big_step(ring, j, k):
        ring.wait(k)
        if k + 1 < ring.steps:
            ring.send(k + 1)
            for d in (0, 1):
                share(j, ring.region(ring.origin(d, k + 1), None))
        else:
            share(j, ring.region(ring.origin(0, k + 1), None))

    def multiply(j):
        part[j] = jnp.dot(cot_ref[...], slab[j], preferred_element_type=F32)

    def rs_copy(j, s):
        return pltpu.make_async_remote_copy(
            src_ref=snd.at[j], dst_ref=(fr_l if s > 0 else fr_r).at[j],
            send_sem=rs_s.at[j], recv_sem=(rl_r if s > 0 else rr_r).at[j],
            device_id=(f, t + s), device_id_type=MESH,
        )

    def rs_wait(j, s):
        ref, sem = (fr_l, rl_r) if s > 0 else (fr_r, rr_r)
        pltpu.make_async_remote_copy(
            src_ref=snd.at[j], dst_ref=ref.at[j], send_sem=rs_s.at[j], recv_sem=sem.at[j],
            device_id=(f, t), device_id_type=MESH,
        ).wait_recv()

    def slot(n):
        for s in (1, -1):
            for stage in range(3):
                hop = n - 2 * stage
                if not 0 <= hop < NT - 1:
                    continue
                at = hop if s > 0 else NT - 1 - hop
                dests = [j for j in (5 - stage, stage) if (j - at) * s > 0]
                if not dests:
                    continue

                @pl.when(t == at)
                def _():
                    for j in dests:
                        if hop > 0:
                            rs_wait(j, s)
                            snd[j] = (part[j] + (fr_l if s > 0 else fr_r)[j].astype(F32)).astype(BF16)
                        else:
                            snd[j] = part[j].astype(BF16)
                        rs_copy(j, s).start()

    def project(js):
        acc = None
        for j in js:
            d = lax.dot_general(att[j], slab[j], NT_DIMS, preferred_element_type=F32)
            acc = d if acc is None else acc + d
        return acc

    for j in range(NT):
        v = c * 32 + (y2 * 4 + x if j >= 3 else x * 8 + y2)
        mine = slab.at[j, pl.ds(pl.multiple_of(v * UNIT, UNIT), UNIT), :]
        pltpu.make_async_remote_copy(
            src_ref=mine, dst_ref=mine, send_sem=pre_s.at[0], recv_sem=pre_r.at[j],
            device_id=(f, t), device_id_type=MESH,
        ).wait_recv()

    ax.send(0)
    by.send(0)
    ax.wait(0)
    ax.send(1)
    by.wait(0)
    by.send(1)
    att_step(1)
    ax.wait(1)
    ay[0].send(0)
    ay[1].send(0)
    for s in range(3):
        share(5 - s, big_a(5 - s, y, None))
    by.wait(1)
    by.send(2)
    big_step(ay[0], 5, 0)
    by.wait(2)
    by.send(3)
    att_step(2)
    big_step(ay[1], 4, 0)
    by.wait(3)
    bx[0].send(0)
    bx[1].send(0)
    for s in range(3):
        share(s, big_b(s, x, None))
    big_step(ay[0], 5, 1)
    big_step(ay[1], 4, 1)
    big_step(bx[0], 0, 0)
    big_step(ay[0], 5, 2)
    att_step(3)
    big_step(bx[0], 0, 1)
    big_step(ay[1], 4, 2)
    ay[2].send(0)
    big_step(bx[1], 1, 0)
    bx[2].send(0)
    big_step(ay[0], 5, 3)
    shared(0)
    shared(5)
    multiply(5)
    multiply(0)
    slot(0)
    big_step(ay[2], 3, 0)
    big_step(bx[1], 1, 1)
    big_step(ay[1], 4, 3)
    att_step(4)
    slot(1)
    big_step(ay[2], 3, 1)
    big_step(bx[2], 2, 0)
    shared(1)
    shared(4)
    multiply(4)
    multiply(1)
    slot(2)
    big_step(ay[2], 3, 2)
    big_step(bx[2], 2, 1)
    slot(3)
    big_step(ay[2], 3, 3)
    shared(2)
    shared(3)
    multiply(3)
    multiply(2)
    slot(4)
    att_step(5)
    total = project((0, 1, 2))
    slot(5)
    total = total + project((3, 4, 5))
    proj_ref[...] = total.astype(BF16)
    slot(6)

    @pl.when(t > 0)
    def _():
        rs_wait(t, 1)
        part[t] += fr_l[t].astype(F32)

    @pl.when(t < NT - 1)
    def _():
        rs_wait(t, -1)
        part[t] += fr_r[t].astype(F32)

    for h in range(4):
        cols = slice(h * HD, (h + 1) * HD)
        qh, kh, vh = q_ref[:, cols], k_ref[:, cols], v_ref[:, cols]
        g = part[t, :, cols].astype(BF16)
        p = probs[h]
        gv_ref[:, cols] = lax.dot_general(p.astype(BF16), g, TN_DIMS, preferred_element_type=F32).astype(BF16)
        gp = lax.dot_general(g, vh, NT_DIMS, preferred_element_type=F32)
        delta = jnp.sum(gp * p, axis=-1, keepdims=True)
        gs = (p * (gp - delta) * SCALE).astype(BF16)
        gq_ref[:, cols] = jnp.dot(gs, kh, preferred_element_type=F32).astype(BF16)
        gk_ref[:, cols] = lax.dot_general(gs, qh, TN_DIMS, preferred_element_type=F32).astype(BF16)

    for i in range(3):
        for z in (0, 1):
            pre_copy(i, z).wait_send()
    for ring in [ax, by] + ay + bx:
        ring.finish()
    for _, cp in to_sib:
        cp.wait_send()
    for k in range(NT - 1):
        for s in (1, -1):
            has = (t >= k) if s > 0 else (t + k <= NT - 1)
            room = (t < NT - 1) if s > 0 else (t > 0)

            @pl.when(has & room)
            def _():
                att_copy(t - s * k, s, k).wait_send()
    for j in range(NT):
        @pl.when(t != j)
        def _():
            rs_copy(j, 1).wait_send()


def shards(queries, keys, values, out_weight, cotangent, image_ids):
    tok, width = queries.shape
    vmem = pl.BlockSpec(memory_space=pltpu.VMEM)
    dma = pltpu.SemaphoreType.DMA
    grads = jax.ShapeDtypeStruct((tok, width), BF16)
    return pl.pallas_call(
        kernel,
        out_shape=(jax.ShapeDtypeStruct(cotangent.shape, BF16), grads, grads, grads),
        in_specs=[vmem] * 6,
        out_specs=(vmem,) * 4,
        scratch_shapes=[
            pltpu.VMEM((NT, 1024, 512), BF16),
            pltpu.VMEM((NT, tok, width), BF16),
            pltpu.VMEM((NT, tok, width), BF16),
            pltpu.VMEM((NT, tok, width), BF16),
            pltpu.VMEM((NT, tok, width), BF16),
            pltpu.VMEM((NT, tok, width), F32),
            pltpu.VMEM((4, tok, tok), F32),
            dma((6,)), dma((6,)),
            dma((4,)), dma((4,)),
            dma((8,)), dma((8,)),
            dma((3, 8)), dma((3, 8)),
            dma((3, 4)), dma((3, 4)),
            dma((6, 8)), dma((6,)),
            dma((5,)), dma((5,)), dma((6,)),
            dma((6,)), dma((6,)), dma((6,)),
        ],
        compiler_params=pltpu.CompilerParams(
            collective_id=0, has_side_effects=True, vmem_limit_bytes=48 * 1024 * 1024
        ),
        name="attention",
    )(queries, keys, values, out_weight.T, cotangent, image_ids)


def solution(mesh):
    return jax.shard_map(
        shards,
        mesh=mesh,
        in_specs=(
            P("fsdp", "tensor"),
            P("fsdp", "tensor"),
            P("fsdp", "tensor"),
            P("tensor", "fsdp"),
            P("fsdp", "tensor"),
            P("fsdp", None),
        ),
        out_specs=(
            P("fsdp", "tensor"),
            P("fsdp", "tensor"),
            P("fsdp", "tensor"),
            P("fsdp", "tensor"),
        ),
        check_vma=False,
    )
```

time: 314 us -> 102 us (0.32)
  the two profiles are of different devices: /device:TPU:6 before, /device:TPU:128 now
where the time goes in v1:
time: 102 us
  Pallas kernels  93.1 us (91%)
  local copies, waits for them, and re-layouts  7.78 us (8%)
    pallas_call x1, Pallas kernels, shards(): pl.pallas_call(kernel, out_shape=(jax.ShapeDtypeStruct(cotangent.shape, B...  93.1 us
    unnamed x16, local copies, waits for them, and re-layouts  7.78 us

profile of v1, /device:TPU:128, one launch (start us, length us, event | category | flops | bytes accessed | tf_op | source)
XLA Modules:
  0.0 101.6 jit_solution(5789797976172259711)
XLA Ops:
  0.6 0.0 copy-start.5
  0.6 0.6 copy-done.5
  1.3 0.0 copy-start
  1.3 0.9 copy-done
  2.2 0.0 copy-start.1
  2.2 0.9 copy-done.1
  3.1 0.0 copy-start.2
  3.1 0.9 copy-done.2
  4.0 0.0 copy-start.3
  4.1 0.9 copy-done.3
  5.0 0.0 copy-start.4
  5.0 0.8 copy-done.4
  5.8 93.1 %attention.1 = (bf16[128,1024]{1,0:T(8,128)(2,1)S(1)}, bf16[128,512]{1,0:T(8,128)(2,1)S(1)}, bf16[128,512]{1,0:T(8,128)(2,1)S(1)}, bf16[128,512]{1,0:T(8,128)(2,1)S(1)}) custom-call(bf16[128,512]{1,0:T(8,128)(2,1)S(1)} %copy-done.1, bf16[128,512]{1,0:T(8,128)(2,1)S(1)} %copy-done.2, bf16[128,512]{1,0:T(8,128)(2,1)S(1)} %copy-done.3, ...), custom_call_target="tpu_custom_call" | custom-call | tf_op jit(solution)/shard_map/attention/pallas_call | solution.py:402
  98.9 0.7 copy.14
  99.6 0.7 copy.15
  100.2 0.7 copy.16
  100.9 0.7 copy.17
Async XLA Ops:
  0.6 0.7 copy-start.5
  1.3 0.9 copy-start
  2.2 0.9 copy-start.1
  3.1 0.9 copy-start.2
  4.0 0.9 copy-start.3
  5.0 0.8 copy-start.4

commit v2 on v1

v2 whole, which is shorter than its diff:
```python
import functools

import jax
import jax.numpy as jnp
from jax import lax
from jax.experimental import pallas as pl
from jax.experimental.pallas import tpu as pltpu
from jax.sharding import PartitionSpec as P

HD = 128
HALF = 2 * HD
SCALE = HD ** (-0.5)
MESH = pl.DeviceIdType.MESH
NX, NY, NT = 4, 8, 6
UNIT = 16
F32 = jnp.float32
BF16 = jnp.bfloat16

NT_DIMS = (((1,), (1,)), ((), ()))
TN_DIMS = (((0,), (0,)), ((), ()))


def mod(a, n):
    return lax.rem(a + 4 * n, n)


def shift_of(slab):
    return 3 - slab % 3


def coords(f):
    return f // 16, (f // 4) % 4, (f // 2) % 2, f % 2


def index_of(y, x, zh, c):
    return ((y * NX + x) * 2 + zh) * 2 + c


class Ring:
    def __init__(self, n, pos, device, region, send_sem, recv_sem):
        self.n, self.pos, self.device, self.region = n, pos, device, region
        self.send_sem, self.recv_sem = send_sem, recv_sem
        self.steps = n // 2

    def copy(self, d, k, origin):
        last = k == self.steps - 1
        ref = self.region(origin, d if last else None)
        i = d * self.steps + k
        return pltpu.make_async_remote_copy(
            src_ref=ref, dst_ref=ref,
            send_sem=self.send_sem(i), recv_sem=self.recv_sem(i),
            device_id=self.device(1 if d == 0 else -1), device_id_type=MESH,
        )

    def origin(self, d, k):
        return mod(self.pos - k if d == 0 else self.pos + k, self.n)

    def send(self, k):
        for d in (0, 1):
            self.copy(d, k, self.origin(d, k)).start()

    def wait(self, k):
        for d in (0, 1):
            self.copy(d, k, self.origin(d, k + 1)).wait_recv()

    def finish(self):
        for k in range(self.steps):
            for d in (0, 1):
                self.copy(d, k, self.origin(d, k)).wait_send()


def kernel(q_hbm, k_hbm, v_hbm, wt_ref, cot_hbm, ids_hbm,
           proj_hbm, gq_hbm, gk_hbm, gv_hbm,
           proj_ref, gq_ref, gk_ref, gv_ref, q_ref, k_ref, v_ref, cot_ref, ids_ref,
           slab, att, fr, snd, part, probs, in_sem, out_sem,
           pre_s, pre_r, ax_s, ax_r, by_s, by_r, ay_s, ay_r, bx_s, bx_r,
           dd_s, dd_r, zr_s, zl_s, za_r, rs_s, rs_r):
    f = lax.axis_index("fsdp")
    t = lax.axis_index("tensor")
    y, x, zh, c = coords(f)
    turn = shift_of(t)
    y2 = lax.rem(y + turn, NY)
    x2 = lax.rem(x + turn, NX)
    in_a = t // 3

    sib = f + 1 - 2 * c
    x_dev = lambda s: (index_of(y, mod(x + s, NX), zh, c), t)
    y_dev = lambda s: (index_of(mod(y + s, NY), x, zh, c), t)

    loads = [
        pltpu.make_async_copy(src, dst, in_sem.at[i])
        for i, (src, dst) in enumerate((
            (ids_hbm, ids_ref), (q_hbm, q_ref), (k_hbm, k_ref), (v_hbm, v_ref), (cot_hbm, cot_ref)))
    ]
    for load in loads:
        load.start()

    barrier = pltpu.get_barrier_semaphore()

    def greet(device):
        pl.semaphore_signal(barrier, inc=1, device_id=device, device_id_type=MESH)

    def units(j):
        if j >= 3:
            return [c * 32 + y2 * 4 + x2]
        return [c * 32 + x2 * 8 + y2, c * 32 + x2 * 8 + lax.rem(y2 + 4, NY)]

    for j in range(NT):
        for v in units(j):
            greet(((64 * t + v) // 3, j))
    for s in (1, -1, 2):
        greet(x_dev(s))
    for s in (1, -1, 2, -2):
        greet(y_dev(s))
    greet((sib, t))

    @pl.when(t > 0)
    def _():
        greet((f, t - 1))

    @pl.when(t < NT - 1)
    def _():
        greet((f, t + 1))

    @pl.when((t == 3) | (t == 5))
    def _():
        greet((f, t - 2))

    @pl.when((t == 0) | (t == 2))
    def _():
        greet((f, t + 2))

    inner = ((t + NT - 1) // NT) * ((2 * NT - 2 - t) // NT)
    pl.semaphore_wait(barrier, 12 - 6 * in_a + 8 + 1 + 2 * inner)

    def pre_copy(i, z, h):
        u = 3 * f + i
        to = u // 64
        v = u % 64
        rest = v % 32
        ya, xa = rest // 4, rest % 4
        yb, xb = rest % 8, rest // 8
        yy = in_a * ya + (1 - in_a) * yb
        xx = in_a * xa + (1 - in_a) * xb
        yd = lax.rem(yy - shift_of(to) + 4 * h + NY, NY)
        xd = lax.rem(xx - shift_of(to) + NX, NX)
        return pltpu.make_async_remote_copy(
            src_ref=wt_ref.at[pl.ds(i * UNIT, UNIT), :],
            dst_ref=slab.at[t, pl.ds(pl.multiple_of(v * UNIT, UNIT), UNIT), :],
            send_sem=pre_s.at[(2 * i + z) * 2 + h], recv_sem=pre_r.at[h, t],
            device_id=(index_of(yd, xd, z, v // 32), to), device_id_type=MESH,
        )

    def pre_all(act):
        @pl.when(t < 3)
        def _():
            for i in range(3):
                for z in (0, 1):
                    for h in (0, 1):
                        act(pre_copy(i, z, h))

        @pl.when(t >= 3)
        def _():
            for i in range(3):
                for z in (0, 1):
                    act(pre_copy(i, z, 0))

    pre_all(lambda cp: cp.start())

    for load in loads:
        load.wait()

    ids_row = jnp.broadcast_to(ids_ref[...].astype(F32), (HD, HD))
    same = ids_row == ids_row.T
    for h in range(4):
        cols = slice(h * HD, (h + 1) * HD)
        s = lax.dot_general(q_ref[:, cols], k_ref[:, cols], NT_DIMS, preferred_element_type=F32) * SCALE
        s = jnp.where(same, s, -1e30)
        w = jnp.exp(s - jnp.max(s, axis=-1, keepdims=True))
        p = w / jnp.sum(w, axis=-1, keepdims=True)
        probs[h] = p
        a = jnp.dot(p.astype(BF16), v_ref[:, cols], preferred_element_type=F32)
        att[t, :, cols] = a.astype(BF16)

    def att_copy(block, s, k):
        return pltpu.make_async_remote_copy(
            src_ref=att.at[block], dst_ref=att.at[block],
            send_sem=(zr_s if s > 0 else zl_s).at[k], recv_sem=za_r.at[block],
            device_id=(f, t + s), device_id_type=MESH,
        )

    def att_wait(block):
        pltpu.make_async_remote_copy(
            src_ref=att.at[block], dst_ref=att.at[block],
            send_sem=zr_s.at[0], recv_sem=za_r.at[block],
            device_id=(f, t), device_id_type=MESH,
        ).wait_recv()

    def att_step(k):
        for s in (1, -1):
            block = t - s * k
            has = (t >= k) if s > 0 else (t + k <= NT - 1)
            room = (t < NT - 1) if s > 0 else (t > 0)
            if k > 0:
                @pl.when(has)
                def _():
                    att_wait(block)
            if k < NT - 1:
                @pl.when(has & room)
                def _():
                    att_copy(block, s, k).start()

    att_step(0)

    def small_a(o, half):
        r = pl.ds(pl.multiple_of(c * 512 + y2 * 64 + lax.rem(o + turn, NX) * UNIT, UNIT), UNIT)
        w = slice(None) if half is None else pl.ds(half * 256, 256)
        return slab.at[pl.ds(3, 3), r, w]

    def small_b(o, half):
        r = pl.ds(pl.multiple_of(c * 512 + x2 * 128 + lax.rem(o + turn, NY) * UNIT, UNIT), UNIT)
        w = slice(None) if half is None else pl.ds(half * 256, 256)
        return slab.at[pl.ds(0, 3), r, w]

    def big_a(j, o, half):
        r = pl.ds(pl.multiple_of(c * 512 + lax.rem(o + turn, NY) * 64, 64), 64)
        w = slice(None) if half is None else pl.ds(half * 256, 256)
        return slab.at[j, r, w]

    def big_b(j, o, half):
        r = pl.ds(pl.multiple_of(c * 512 + lax.rem(o + turn, NX) * 128, 128), 128)
        w = slice(None) if half is None else pl.ds(half * 256, 256)
        return slab.at[j, r, w]

    def sender(region, device, ssem, rsem):
        def copy(i, s, o, half):
            ref = region(o, half)
            return pltpu.make_async_remote_copy(
                src_ref=ref, dst_ref=ref, send_sem=ssem.at[i], recv_sem=rsem.at[i],
                device_id=device(s), device_id_type=MESH,
            )
        return copy

    ax = sender(small_a, x_dev, ax_s, ax_r)
    by = sender(small_b, y_dev, by_s, by_r)
    ax_plan = [(i, s, 0, None) for i, s in enumerate((1, -1, 2))]
    by_plan = [(0, 1, 0, None), (1, -1, 0, None), (2, 2, 0, None), (3, -2, 0, None), (4, 1, 4, None), (5, -1, 4, None)]

    def go(copy, pos, n, plan):
        for i, s, o, half in plan:
            copy(i, s, mod(pos + o, n), half).start()

    def come(copy, pos, n, plan):
        for i, s, o, half in plan:
            copy(i, s, mod(pos - s + o, n), half).wait_recv()

    def gone(copy, pos, n, plan):
        for i, s, o, half in plan:
            copy(i, s, mod(pos + o, n), half).wait_send()

    ay = [Ring(NY, y, y_dev, functools.partial(big_a, 5 - s),
               lambda i, s=s: ay_s.at[s, i], lambda i, s=s: ay_r.at[s, i]) for s in range(3)]
    bx = [Ring(NX, x, x_dev, functools.partial(big_b, s),
               lambda i, s=s: bx_s.at[s, i], lambda i, s=s: bx_r.at[s, i]) for s in range(3)]

    to_sib = []

    def share(j, ref):
        i = sum(1 for jj, _ in to_sib if jj == j)
        cp = pltpu.make_async_remote_copy(
            src_ref=ref, dst_ref=ref, send_sem=dd_s.at[j, i], recv_sem=dd_r.at[j],
            device_id=(sib, t), device_id_type=MESH,
        )
        cp.start()
        to_sib.append((j, cp))

    def shared(j):
        half = slab.at[j, pl.ds(pl.multiple_of((1 - c) * 512, 512), 512), :]
        pltpu.make_async_remote_copy(
            src_ref=half, dst_ref=half, send_sem=dd_s.at[j, 0], recv_sem=dd_r.at[j],
            device_id=(sib, t), device_id_type=MESH,
        ).wait_recv()

    def big_step(ring, j, k):
        ring.wait(k)
        if k + 1 < ring.steps:
            ring.send(k + 1)
            for d in (0, 1):
                share(j, ring.region(ring.origin(d, k + 1), None))
        else:
            share(j, ring.region(ring.origin(0, k + 1), None))

    def multiply(j):
        part[j] = jnp.dot(cot_ref[...], slab[j], preferred_element_type=F32)

    SIDES = (-1, -2, 1, 2)

    def rs_copy(j, s, b):
        i = SIDES.index(-s)
        cols = pl.ds(b * HALF, HALF)
        return pltpu.make_async_remote_copy(
            src_ref=snd.at[j, :, cols], dst_ref=fr.at[i, j, :, cols],
            send_sem=rs_s.at[b, j], recv_sem=rs_r.at[b, i, j],
            device_id=(f, t + s), device_id_type=MESH,
        )

    def rs_take(j, s, b):
        i = SIDES.index(s)
        cols = pl.ds(b * HALF, HALF)
        pltpu.make_async_remote_copy(
            src_ref=snd.at[j, :, cols], dst_ref=fr.at[i, j, :, cols],
            send_sem=rs_s.at[b, j], recv_sem=rs_r.at[b, i, j],
            device_id=(f, t), device_id_type=MESH,
        ).wait_recv()
        return fr[i, j, :, b * HALF:(b + 1) * HALF].astype(F32)

    def gather_in(j, takes, b):
        total = part[j, :, b * HALF:(b + 1) * HALF]
        for q in takes:
            total = total + rs_take(j, q, b)
        snd[j, :, b * HALF:(b + 1) * HALF] = total.astype(BF16)

    def step_of(at, j):
        flip = j < at
        a, d = (NT - 1 - at, NT - 1 - j) if flip else (at, j)
        takes, to = {
            0: ((), 1),
            1: ((-1,), 3 if d >= 3 else 2),
            2: ((), 3),
            3: ((-1, -2), 4 if d == 4 else 5),
            4: ((), 5),
        }[a]
        sign = -1 if flip else 1
        return tuple(sign * q for q in takes), sign * (to - a)

    def first(j):
        for at in range(NT):
            if at != j and not step_of(at, j)[0]:
                @pl.when(t == at)
                def _():
                    for b in (0, 1):
                        gather_in(j, (), b)
                        rs_copy(j, step_of(at, j)[1], b).start()

    def later(js):
        for at in range(NT):
            mine = [j for j in js if j != at and step_of(at, j)[0]]
            if mine:
                @pl.when(t == at)
                def _():
                    for j in mine:
                        takes, to = step_of(at, j)
                        for b in (0, 1):
                            gather_in(j, takes, b)
                            rs_copy(j, to, b).start()

    LAST = {0: (1, 2), 1: (-1, 1), 2: (-1, 1, 2), 3: (-1, -2, 1), 4: (-1, 1), 5: (-1, -2)}

    def last(b):
        for at in range(NT):
            @pl.when(t == at)
            def _():
                gather_in(at, LAST[at], b)

    def sent():
        for at in range(NT):
            @pl.when(t == at)
            def _():
                for j in range(NT):
                    if j != at:
                        for b in (0, 1):
                            rs_copy(j, step_of(at, j)[1], b).wait_send()

    def project(js):
        acc = None
        for j in js:
            d = lax.dot_general(att[j], slab[j], NT_DIMS, preferred_element_type=F32)
            acc = d if acc is None else acc + d
        return acc

    for j in range(NT):
        for h, v in enumerate(units(j)):
            mine = slab.at[j, pl.ds(pl.multiple_of(v * UNIT, UNIT), UNIT), :]
            pltpu.make_async_remote_copy(
                src_ref=mine, dst_ref=mine, send_sem=pre_s.at[0], recv_sem=pre_r.at[h, j],
                device_id=(f, t), device_id_type=MESH,
            ).wait_recv()

    go(ax, x, NX, ax_plan)
    go(by, y, NY, by_plan)
    att_step(1)
    come(ax, x, NX, ax_plan)
    for s in range(3):
        ay[s].send(0)
    come(by, y, NY, by_plan)
    for s in range(3):
        bx[s].send(0)
    for s in range(3):
        share(5 - s, big_a(5 - s, y, None))
    for s in range(3):
        share(s, big_b(s, x, None))
    att_step(2)
    for s in range(3):
        big_step(ay[s], 5 - s, 0)
    big_step(bx[0], 0, 0)
    big_step(ay[0], 5, 1)
    big_step(bx[1], 1, 0)
    big_step(ay[1], 4, 1)
    big_step(bx[2], 2, 0)
    big_step(ay[2], 3, 1)
    att_step(3)
    big_step(bx[0], 0, 1)
    big_step(ay[0], 5, 2)
    big_step(ay[1], 4, 2)
    big_step(ay[2], 3, 2)
    big_step(bx[1], 1, 1)
    shared(0)
    multiply(0)
    first(0)
    att_step(4)
    for s in range(3):
        big_step(ay[s], 5 - s, 3)
    big_step(bx[2], 2, 1)
    for j in (5, 1, 4, 3, 2):
        shared(j)
        multiply(j)
        first(j)

    pre_all(lambda cp: cp.wait_send())
    gone(ax, x, NX, ax_plan)
    gone(by, y, NY, by_plan)
    for ring in ay + bx:
        ring.finish()
    for _, cp in to_sib:
        cp.wait_send()

    later((0, 5))
    att_step(5)
    total = project((0, 1, 2))
    later((1, 4))
    total = total + project((3, 4, 5))
    proj_ref[...] = total.astype(BF16)
    stores = [
        pltpu.make_async_copy(src, dst, out_sem.at[i])
        for i, (src, dst) in enumerate((
            (proj_ref, proj_hbm), (gq_ref, gq_hbm), (gk_ref, gk_hbm), (gv_ref, gv_hbm)))
    ]
    stores[0].start()
    later((3, 2))

    for h in range(4):
        if h % 2 == 0:
            last(h // 2)
        cols = slice(h * HD, (h + 1) * HD)
        qh, kh, vh = q_ref[:, cols], k_ref[:, cols], v_ref[:, cols]
        g = snd[t, :, cols]
        p = probs[h]
        gv_ref[:, cols] = lax.dot_general(p.astype(BF16), g, TN_DIMS, preferred_element_type=F32).astype(BF16)
        gp = lax.dot_general(g, vh, NT_DIMS, preferred_element_type=F32)
        delta = jnp.sum(gp * p, axis=-1, keepdims=True)
        gs = (p * (gp - delta) * SCALE).astype(BF16)
        gq_ref[:, cols] = jnp.dot(gs, kh, preferred_element_type=F32).astype(BF16)
        gk_ref[:, cols] = lax.dot_general(gs, qh, TN_DIMS, preferred_element_type=F32).astype(BF16)
    for store in stores[1:]:
        store.start()

    for k in range(NT - 1):
        for s in (1, -1):
            has = (t >= k) if s > 0 else (t + k <= NT - 1)
            room = (t < NT - 1) if s > 0 else (t > 0)

            @pl.when(has & room)
            def _():
                att_copy(t - s * k, s, k).wait_send()
    sent()
    for store in stores:
        store.wait()


def hand_over(*refs):
    srcs, dsts, bufs, sems = refs[:4], refs[4:8], refs[8:12], refs[12]
    loads = [pltpu.make_async_copy(srcs[i], bufs[i], sems.at[0, i]) for i in range(4)]
    stores = [pltpu.make_async_copy(bufs[i], dsts[i], sems.at[1, i]) for i in range(4)]
    for load in loads:
        load.start()
    for load, store in zip(loads, stores):
        load.wait()
        store.start()
    for store in stores:
        store.wait()


def shards(queries, keys, values, out_weight, cotangent, image_ids):
    tok, width = queries.shape
    anywhere = pl.BlockSpec(memory_space=pl.ANY)
    dma = pltpu.SemaphoreType.DMA
    grads = jax.ShapeDtypeStruct((tok, width), BF16)
    outs = (jax.ShapeDtypeStruct(cotangent.shape, BF16), grads, grads, grads)
    results = pl.pallas_call(
        kernel,
        out_shape=outs,
        in_specs=[anywhere] * 6,
        out_specs=(anywhere,) * 4,
        scratch_shapes=[
            pltpu.VMEM(cotangent.shape, BF16),
            pltpu.VMEM((tok, width), BF16),
            pltpu.VMEM((tok, width), BF16),
            pltpu.VMEM((tok, width), BF16),
            pltpu.VMEM((tok, width), BF16),
            pltpu.VMEM((tok, width), BF16),
            pltpu.VMEM((tok, width), BF16),
            pltpu.VMEM(cotangent.shape, BF16),
            pltpu.VMEM(image_ids.shape, image_ids.dtype),
            pltpu.VMEM((NT, 1024, 512), BF16),
            pltpu.VMEM((NT, tok, width), BF16),
            pltpu.VMEM((4, NT, tok, width), BF16),
            pltpu.VMEM((NT, tok, width), BF16),
            pltpu.VMEM((NT, tok, width), F32),
            pltpu.VMEM((4, tok, tok), F32),
            dma((5,)), dma((4,)),
            dma((12,)), dma((2, 6)),
            dma((3,)), dma((3,)),
            dma((6,)), dma((6,)),
            dma((3, 8)), dma((3, 8)),
            dma((3, 4)), dma((3, 4)),
            dma((6, 8)), dma((6,)),
            dma((5,)), dma((5,)), dma((6,)),
            dma((2, 6)), dma((2, 4, 6)),
        ],
        compiler_params=pltpu.CompilerParams(
            collective_id=0, has_side_effects=True, vmem_limit_bytes=60 * 1024 * 1024
        ),
        name="attention",
    )(queries, keys, values, out_weight.T, cotangent, image_ids)
    return pl.pallas_call(
        hand_over,
        out_shape=outs,
        in_specs=[anywhere] * 4,
        out_specs=(anywhere,) * 4,
        scratch_shapes=[pltpu.VMEM(out.shape, BF16) for out in outs] + [dma((2, 4))],
        compiler_params=pltpu.CompilerParams(vmem_limit_bytes=60 * 1024 * 1024),
        name="hand_over",
    )(*results)


def solution(mesh):
    return jax.shard_map(
        shards,
        mesh=mesh,
        in_specs=(
            P("fsdp", "tensor"),
            P("fsdp", "tensor"),
            P("fsdp", "tensor"),
            P("tensor", "fsdp"),
            P("fsdp", "tensor"),
            P("fsdp", None),
        ),
        out_specs=(
            P("fsdp", "tensor"),
            P("fsdp", "tensor"),
            P("fsdp", "tensor"),
            P("fsdp", "tensor"),
        ),
        check_vma=False,
    )
```

time: 102 us -> 85.5 us (0.84)
  Pallas kernels: 93.1 us -> 84.7 us
  local copies, waits for them, and re-layouts: 7.78 us -> 0 us
    pallas_call x1 -> x2, Pallas kernels: 93.1 us -> 84.7 us  [the longest x1 82.9 us: shards(): pl.pallas_call(kernel, out_shape=outs, in_specs=[anywhere] * 6, out_specs...]
    unnamed x16 -> x0, local copies, waits for them, and re-layouts: 7.78 us -> none
where the time goes in v2:
time: 85.5 us; the launch traced here: 85.4 us
  Pallas kernels  84.7 us (99%)
    pallas_call x1, Pallas kernels, shards(): pl.pallas_call(kernel, out_shape=outs, in_specs=[anywhere] * 6, out_specs...  82.9 us
    pallas_call x1, Pallas kernels, shards(): pl.pallas_call(hand_over, out_shape=outs, in_specs=[anywhere] * 4, out_sp...  1.85 us

profile of v2, /device:TPU:128, one launch (start us, length us, event | category | flops | bytes accessed | tf_op | source)
XLA Modules:
  0.0 85.4 jit_solution(17058603822788785252)
XLA Ops:
  0.6 82.9 %attention.1 = (bf16[128,1024]{1,0:T(8,128)(2,1)}, bf16[128,512]{1,0:T(8,128)(2,1)}, bf16[128,512]{1,0:T(8,128)(2,1)}, bf16[128,512]{1,0:T(8,128)(2,1)}) custom-call(bf16[128,512]{1,0:T(8,128)(2,1)} %q_hbm.1, bf16[128,512]{1,0:T(8,128)(2,1)} %k_hbm.1, bf16[128,512]{1,0:T(8,128)(2,1)} %v_hbm.1, bf16[48,512]{1,0:T(8,128)(2,1)} %bitcast.1, ...), custom_call_target="tpu_custom_call" | custom-call | tf_op jit(solution)/shard_map/attention/pallas_call | solution.py:499
  83.5 1.8 %hand_over.1 = (bf16[128,1024]{1,0:T(8,128)(2,1)}, bf16[128,512]{1,0:T(8,128)(2,1)}, bf16[128,512]{1,0:T(8,128)(2,1)}, bf16[128,512]{1,0:T(8,128)(2,1)}) custom-call(bf16[128,1024]{1,0:T(8,128)(2,1)} %get-tuple-element.8.refs_0_, bf16[128,512]{1,0:T(8,128)(2,1)} %get-tuple-element.9.refs_1_, bf16[128,512]{1,0:T(8,128)(2,1)} %get-tuple-element.10.refs_2_, ...), custom_call_target="tpu_custom_call" | custom-call | tf_op jit(solution)/shard_map/hand_over/pallas_call | solution.py:535

commit v3 on v2

--- a/solution.py
+++ b/solution.py
@@ -13,6 +13,8 @@
 MESH = pl.DeviceIdType.MESH
 NX, NY, NT = 4, 8, 6
 UNIT = 16
+AY, BX = (1, 3, 4), (0, 2, 5)
+PLACE = (0, 3, 1, 4, 5, 2)
 F32 = jnp.float32
 BF16 = jnp.bfloat16
 
@@ -81,7 +83,8 @@
     turn = shift_of(t)
     y2 = lax.rem(y + turn, NY)
     x2 = lax.rem(x + turn, NX)
-    in_a = t // 3
+    in_a = (t % 3) % 2 + (t // 3) * (1 - (t % 3 + 1) // 2)
+    place = in_a * (t - t // 3 + 2) + (1 - in_a) * (t // 2)
 
     sib = f + 1 - 2 * c
     x_dev = lambda s: (index_of(y, mod(x + s, NX), zh, c), t)
@@ -101,7 +104,7 @@
         pl.semaphore_signal(barrier, inc=1, device_id=device, device_id_type=MESH)
 
     def units(j):
-        if j >= 3:
+        if j in AY:
             return [c * 32 + y2 * 4 + x2]
         return [c * 32 + x2 * 8 + y2, c * 32 + x2 * 8 + lax.rem(y2 + 4, NY)]
 
@@ -146,20 +149,20 @@
         xd = lax.rem(xx - shift_of(to) + NX, NX)
         return pltpu.make_async_remote_copy(
             src_ref=wt_ref.at[pl.ds(i * UNIT, UNIT), :],
-            dst_ref=slab.at[t, pl.ds(pl.multiple_of(v * UNIT, UNIT), UNIT), :],
+            dst_ref=slab.at[place, pl.ds(pl.multiple_of(v * UNIT, UNIT), UNIT), :],
             send_sem=pre_s.at[(2 * i + z) * 2 + h], recv_sem=pre_r.at[h, t],
             device_id=(index_of(yd, xd, z, v // 32), to), device_id_type=MESH,
         )
 
     def pre_all(act):
-        @pl.when(t < 3)
+        @pl.when(in_a == 0)
         def _():
             for i in range(3):
                 for z in (0, 1):
                     for h in (0, 1):
                         act(pre_copy(i, z, h))
 
-        @pl.when(t >= 3)
+        @pl.when(in_a == 1)
         def _():
             for i in range(3):
                 for z in (0, 1):
@@ -225,12 +228,12 @@
     def big_a(j, o, half):
         r = pl.ds(pl.multiple_of(c * 512 + lax.rem(o + turn, NY) * 64, 64), 64)
         w = slice(None) if half is None else pl.ds(half * 256, 256)
-        return slab.at[j, r, w]
+        return slab.at[PLACE[j], r, w]
 
     def big_b(j, o, half):
         r = pl.ds(pl.multiple_of(c * 512 + lax.rem(o + turn, NX) * 128, 128), 128)
         w = slice(None) if half is None else pl.ds(half * 256, 256)
-        return slab.at[j, r, w]
+        return slab.at[PLACE[j], r, w]
 
     def sender(region, device, ssem, rsem):
         def copy(i, s, o, half):
@@ -258,9 +261,9 @@
         for i, s, o, half in plan:
             copy(i, s, mod(pos + o, n), half).wait_send()
 
-    ay = [Ring(NY, y, y_dev, functools.partial(big_a, 5 - s),
+    ay = [Ring(NY, y, y_dev, functools.partial(big_a, AY[s]),
                lambda i, s=s: ay_s.at[s, i], lambda i, s=s: ay_r.at[s, i]) for s in range(3)]
-    bx = [Ring(NX, x, x_dev, functools.partial(big_b, s),
+    bx = [Ring(NX, x, x_dev, functools.partial(big_b, BX[s]),
                lambda i, s=s: bx_s.at[s, i], lambda i, s=s: bx_r.at[s, i]) for s in range(3)]
 
     to_sib = []
@@ -275,7 +278,7 @@
         to_sib.append((j, cp))
 
     def shared(j):
-        half = slab.at[j, pl.ds(pl.multiple_of((1 - c) * 512, 512), 512), :]
+        half = slab.at[PLACE[j], pl.ds(pl.multiple_of((1 - c) * 512, 512), 512), :]
         pltpu.make_async_remote_copy(
             src_ref=half, dst_ref=half, send_sem=dd_s.at[j, 0], recv_sem=dd_r.at[j],
             device_id=(sib, t), device_id_type=MESH,
@@ -291,7 +294,7 @@
             share(j, ring.region(ring.origin(0, k + 1), None))
 
     def multiply(j):
-        part[j] = jnp.dot(cot_ref[...], slab[j], preferred_element_type=F32)
+        part[j] = jnp.dot(cot_ref[...], slab[PLACE[j]], preferred_element_type=F32)
 
     SIDES = (-1, -2, 1, 2)
 
@@ -374,13 +377,13 @@
     def project(js):
         acc = None
         for j in js:
-            d = lax.dot_general(att[j], slab[j], NT_DIMS, preferred_element_type=F32)
+            d = lax.dot_general(att[j], slab[PLACE[j]], NT_DIMS, preferred_element_type=F32)
             acc = d if acc is None else acc + d
         return acc
 
     for j in range(NT):
         for h, v in enumerate(units(j)):
-            mine = slab.at[j, pl.ds(pl.multiple_of(v * UNIT, UNIT), UNIT), :]
+            mine = slab.at[PLACE[j], pl.ds(pl.multiple_of(v * UNIT, UNIT), UNIT), :]
             pltpu.make_async_remote_copy(
                 src_ref=mine, dst_ref=mine, send_sem=pre_s.at[0], recv_sem=pre_r.at[h, j],
                 device_id=(f, t), device_id_type=MESH,
@@ -393,38 +396,63 @@
     for s in range(3):
         ay[s].send(0)
     come(by, y, NY, by_plan)
-    for s in range(3):
-        bx[s].send(0)
-    for s in range(3):
-        share(5 - s, big_a(5 - s, y, None))
-    for s in range(3):
-        share(s, big_b(s, x, None))
+    bx[0].send(0)
+    bx[1].send(0)
+    for j in AY:
+        share(j, big_a(j, y, None))
+    for j in BX:
+        share(j, big_b(j, x, None))
     att_step(2)
-    for s in range(3):
-        big_step(ay[s], 5 - s, 0)
-    big_step(bx[0], 0, 0)
-    big_step(ay[0], 5, 1)
-    big_step(bx[1], 1, 0)
-    big_step(ay[1], 4, 1)
-    big_step(bx[2], 2, 0)
-    big_step(ay[2], 3, 1)
-    att_step(3)
-    big_step(bx[0], 0, 1)
-    big_step(ay[0], 5, 2)
-    big_step(ay[1], 4, 2)
-    big_step(ay[2], 3, 2)
-    big_step(bx[1], 1, 1)
-    shared(0)
-    multiply(0)
-    first(0)
-    att_step(4)
-    for s in range(3):
-        big_step(ay[s], 5 - s, 3)
-    big_step(bx[2], 2, 1)
-    for j in (5, 1, 4, 3, 2):
+
+    def step_a(s, k):
+        big_step(ay[s], AY[s], k)
+
+    def step_b(s, k):
+        big_step(bx[s], BX[s], k)
+
+    def finish(j):
         shared(j)
         multiply(j)
         first(j)
+
+    step_a(0, 0)
+    step_b(0, 0)
+    step_a(1, 0)
+    step_a(2, 0)
+    step_b(1, 0)
+    bx[2].send(0)
+    step_a(0, 1)
+    step_b(0, 1)
+    step_a(1, 1)
+    att_step(3)
+    step_a(2, 1)
+    finish(BX[0])
+    step_b(1, 1)
+    step_a(0, 2)
+    step_a(1, 2)
+    step_b(2, 0)
+    step_a(2, 2)
+    finish(BX[1])
+    att_step(4)
+    for s in range(3):
+        step_a(s, 3)
+    step_b(2, 1)
+    finish(AY[0])
+    finish(AY[1])
+    finish(AY[2])
+    finish(BX[2])
+    later(BX[:2])
+    later((1, 3))
+    later((4, 5))
+
+    att_step(5)
+    proj_ref[...] = (project((0, 1, 2)) + project((3, 4, 5))).astype(BF16)
+    stores = [
+        pltpu.make_async_copy(src, dst, out_sem.at[i])
+        for i, (src, dst) in enumerate((
+            (proj_ref, proj_hbm), (gq_ref, gq_hbm), (gk_ref, gk_hbm), (gv_ref, gv_hbm)))
+    ]
+    stores[0].start()
 
     pre_all(lambda cp: cp.wait_send())
     gone(ax, x, NX, ax_plan)
@@ -433,20 +461,6 @@
         ring.finish()
     for _, cp in to_sib:
         cp.wait_send()
-
-    later((0, 5))
-    att_step(5)
-    total = project((0, 1, 2))
-    later((1, 4))
-    total = total + project((3, 4, 5))
-    proj_ref[...] = total.astype(BF16)
-    stores = [
-        pltpu.make_async_copy(src, dst, out_sem.at[i])
-        for i, (src, dst) in enumerate((
-            (proj_ref, proj_hbm), (gq_ref, gq_hbm), (gk_ref, gk_hbm), (gv_ref, gv_hbm)))
-    ]
-    stores[0].start()
-    later((3, 2))
 
     for h in range(4):
         if h % 2 == 0:

time: 85.5 us -> 86.6 us (1.013)
  the two profiles are of different devices: /device:TPU:128 before, /device:TPU:64 now
where the time goes in v3:
time: 86.6 us; the launch traced here: 86.5 us
  Pallas kernels  85.8 us (99%)
    pallas_call x1, Pallas kernels, shards(): pl.pallas_call(kernel, out_shape=outs, in_specs=[anywhere] * 6, out_specs...  84 us
    pallas_call x1, Pallas kernels, shards(): pl.pallas_call(hand_over, out_shape=outs, in_specs=[anywhere] * 4, out_sp...  1.85 us

profile of v3, /device:TPU:64, one launch (start us, length us, event | category | flops | bytes accessed | tf_op | source)
XLA Modules:
  0.0 86.5 jit_solution(5255784211207605390)
XLA Ops:
  0.6 84.0 %attention.1 = (bf16[128,1024]{1,0:T(8,128)(2,1)}, bf16[128,512]{1,0:T(8,128)(2,1)}, bf16[128,512]{1,0:T(8,128)(2,1)}, bf16[128,512]{1,0:T(8,128)(2,1)}) custom-call(bf16[128,512]{1,0:T(8,128)(2,1)} %q_hbm.1, bf16[128,512]{1,0:T(8,128)(2,1)} %k_hbm.1, bf16[128,512]{1,0:T(8,128)(2,1)} %v_hbm.1, bf16[48,512]{1,0:T(8,128)(2,1)} %bitcast.1, ...), custom_call_target="tpu_custom_call" | custom-call | tf_op jit(solution)/shard_map/attention/pallas_call | solution.py:513
  84.6 1.8 %hand_over.1 = (bf16[128,1024]{1,0:T(8,128)(2,1)}, bf16[128,512]{1,0:T(8,128)(2,1)}, bf16[128,512]{1,0:T(8,128)(2,1)}, bf16[128,512]{1,0:T(8,128)(2,1)}) custom-call(bf16[128,1024]{1,0:T(8,128)(2,1)} %get-tuple-element.8.refs_0_, bf16[128,512]{1,0:T(8,128)(2,1)} %get-tuple-element.9.refs_1_, bf16[128,512]{1,0:T(8,128)(2,1)} %get-tuple-element.10.refs_2_, ...), custom_call_target="tpu_custom_call" | custom-call | tf_op jit(solution)/shard_map/hand_over/pallas_call | solution.py:549
